TPU v7x, 32 devices: a whole 2x2x4 slice. The times are simulated.
32 devices in a mesh: row: 4 (over y, x), col: 8 (over z, core).
Axes of the slice: x: 2, y: 2, z: 4, core: 2. Of those that a mesh axis runs over, the one named last changes fastest.
Arguments:
- unfolding: float32 [1024, 4096], P('row', 'col'), may hold values from -40 to 40, as said below
- factor: float32 [1024, 64], replicated, may hold values from -6 to 6
Outputs:
- gram_lower: float32 [1024, 1024], P(('row', 'col'))
- new_factor: float32 [1024, 64], replicated
- core: float32 [64, 4096], P('row', 'col')
Inputs may be any that keep to these rules, and one draw needn't show every extreme that they name: Entries of the unfolding are real values.
All inputs are finite; a program needn't handle non-finite values.
Results may differ from a plain program's by a relative error of at most 0.0003.
Values sent between devices are 32-bit elements; how exact they have to be, the bound alone decides.
No kernel may reach another device: no remote copies, remote signals or barrier semaphores. Data moves between devices by JAX's collectives and lax.ppermute only.
A program may use at most 64 MiB of HBM per device.

v0:
```python
import functools
import math

import jax
import jax.numpy as jnp
from jax import lax
from jax.experimental import pallas as pl
from jax.experimental.pallas import tpu as pltpu
from jax.sharding import PartitionSpec as P

F32 = jnp.float32
BF16 = jnp.bfloat16
NN = ((1,), (0,))
NT = ((1,), (1,))


COST = dict(project=10**6, join=10**6, term=10**10, core_sum=10**6, sum=10**6, stack=3 * 10**9, finish=10**10, gram=10**6, pieces=10**6, unpack=10**6)


def tree_sum(parts):
    while len(parts) > 1:
        paired = [a + b for a, b in zip(parts[::2], parts[1::2])]
        parts = paired + parts[2 * len(paired) :]
    return parts[0]


def split2(a):
    hi = a.astype(BF16)
    return hi, (a - hi.astype(F32)).astype(BF16)


def split3(a):
    hi = a.astype(BF16)
    rest = a - hi.astype(F32)
    mid = rest.astype(BF16)
    return hi, mid, (rest - mid.astype(F32)).astype(BF16)


def sided(s, n):
    if n != 4 or s in (0, 3):
        return s
    return jnp.where(lax.axis_index("col") % 2 == 1, 3 - s, s)


def mm(a, b, dims):
    return lax.dot_general(a, b, (dims, ((), ())), preferred_element_type=F32)


def mm3(a, b, dims):
    return mm(a[1], b[0], dims) + mm(a[0], b[1], dims) + mm(a[0], b[0], dims)


def mm4(a, b):
    left = jnp.concatenate([a[0], a[0], a[1], a[1]], 1)
    return mm(left, jnp.concatenate([b[0], b[1], b[0], b[1]], 0), NN)


def gram6(a):
    n = a[0].shape[0]
    s = jnp.concatenate(a, 0)
    g = mm(s, s, NT)

    def at(i, j):
        return g[i * n : (i + 1) * n, j * n : (j + 1) * n]

    return at(0, 0) + ((at(0, 1) + at(1, 0)) + (at(1, 1) + (at(0, 2) + at(2, 0))))


COST = dict(project=10**6, join=10**6, term=10**10, core_sum=10**6, sum=10**6, stack=3 * 10**9, finish=10**10, gram=10**6, pieces=10**6, unpack=10**6)


def tree_sum(parts):
    while len(parts) > 1:
        paired = [a + b for a, b in zip(parts[::2], parts[1::2])]
        parts = paired + parts[2 * len(paired) :]
    return parts[0]


def split2(a):
    hi = a.astype(BF16)
    return hi, (a - hi.astype(F32)).astype(BF16)


def split3(a):
    hi = a.astype(BF16)
    rest = a - hi.astype(F32)
    mid = rest.astype(BF16)
    return hi, mid, (rest - mid.astype(F32)).astype(BF16)


def mm(a, b, dims):
    return lax.dot_general(a, b, (dims, ((), ())), preferred_element_type=F32)


def mm3(a, b, dims):
    return mm(a[1], b[0], dims) + mm(a[0], b[1], dims) + mm(a[0], b[0], dims)


def mm6(a, b, dims):
    low = mm(a[1], b[1], dims) + (mm(a[2], b[0], dims) + mm(a[0], b[2], dims))
    return (low + (mm(a[1], b[0], dims) + mm(a[0], b[1], dims))) + mm(a[0], b[0], dims)


def call(kernel, out_shape, *args, after=(), scratch=(), work=1000, name=None):
    n = len(args)

    def run(*refs):
        kernel(*refs[:n], *refs[n + len(after) :])

    return pl.pallas_call(
        run,
        out_shape=out_shape,
        in_specs=[pl.BlockSpec(memory_space=pltpu.VMEM)] * n + [pl.BlockSpec(memory_space=pl.ANY)] * len(after),
        out_specs=jax.tree.map(lambda _: pl.BlockSpec(memory_space=pltpu.VMEM), out_shape),
        scratch_shapes=list(scratch),
        compiler_params=pltpu.CompilerParams(vmem_limit_bytes=48 * 2**20),
        cost_estimate=pl.CostEstimate(flops=work, bytes_accessed=0, transcendentals=0),
        name=name,
    )(*args, *after)


def project_kernel(rows_here, factor_ref, x_ref, y_ref, *copies):
    row = lax.axis_index("row")
    n_row = factor_ref.shape[1] // rows_here
    mine = factor_ref[:, :rows_here]
    for r in range(1, n_row):
        mine = jnp.where(row == r, factor_ref[:, r * rows_here : (r + 1) * rows_here], mine)
    y_ref[...] = mm3(split2(mine), split2(x_ref[...]), NN)
    for i, ref in enumerate(copies):
        ref[...] = x_ref[i * ref.shape[0] : (i + 1) * ref.shape[0], :]


def join_kernel(mine_ref, got_ref, x_ref, y_ref, copy_ref):
    y_ref[...] = mine_ref[...] + got_ref[...]
    copy_ref[...] = x_ref[...]


def term_kernel(scale, x_ref, mine_ref, got_ref, kept_ref, given_ref):
    core = lax.axis_index("col") % 2
    y = mine_ref[...] + got_ref[...]
    term = mm3(split2(y), split2(x_ref[...]), NT) * scale
    hr = term.shape[0] // 2
    kept_ref[...] = jnp.where(core == 0, term[:hr], term[hr:])
    given_ref[...] = jnp.where(core == 0, term[hr:], term[:hr])


def sum_kernel(mine_ref, got_ref, out_ref):
    out_ref[...] = mine_ref[...] + got_ref[...]


def stack_kernel(mine_ref, got_ref, both_ref):
    n = mine_ref.shape[0]
    both_ref[:n] = mine_ref[...]
    both_ref[n:] = got_ref[...]


def inverse_factor(inner):
    n = inner.shape[0]
    wide = -(-2 * n // 128) * 128
    r = lax.broadcasted_iota(jnp.int32, (n, wide), 0)
    c = lax.broadcasted_iota(jnp.int32, (n, wide), 1)
    w = jnp.where(c == r + n, F32(1.0), F32(0.0))
    w = w + jnp.concatenate([inner, jnp.zeros((n, wide - n), F32)], 1)
    w = [w[8 * i : 8 * i + 8] for i in range(n // 8)]
    sub = lax.broadcasted_iota(jnp.int32, (8, wide), 0)
    done = []
    for b in range(n // 8):
        cols = {
            j: [jnp.broadcast_to(w[i][:, 8 * b + j : 8 * b + j + 1], (8, wide)) for i in range(b, n // 8)]
            for j in range(8)
        }
        for k in range(8):
            pivot = jnp.broadcast_to(cols[k][0][k : k + 1], (8, wide))
            rs = lax.rsqrt(pivot)
            inv = rs * rs
            rs = rs * (1.5 - 0.5 * (pivot * inv))
            inv = inv * (2.0 - pivot * inv)
            row = jnp.broadcast_to(w[b][k : k + 1], (8, wide))
            done.append(row[:1] * rs[:1])
            below = [jnp.where(sub > k, cols[k][0], F32(0.0))] + cols[k][1:]
            m = [a * inv for a in below]
            for j in range(k + 1, 8):
                at = jnp.broadcast_to(cols[j][0][k : k + 1], (8, wide))
                if j == k + 1:
                    cols[j] = [a - (f * at) * inv for a, f in zip(cols[j], below)]
                else:
                    cols[j] = [a - f * at for a, f in zip(cols[j], m)]
            for i in range(b, n // 8):
                w[i] = w[i] - m[i - b] * row
    return jnp.concatenate(done, 0)[:, n : 2 * n]


def finish_kernel(n_row, counts, mine_ref, other_ref, *refs):
    total = sum(counts)
    pieces, (nf_ref, core_ref, rows_ref) = refs[:total], refs[total:]
    row = lax.axis_index("row")
    core = lax.axis_index("col") % 2
    _, hr, rows_here = mine_ref.shape
    rank = 2 * hr
    mode = rows_here * n_row
    blocks = []
    for s in range(n_row):
        mine, other = mine_ref[s], other_ref[s]
        first, second = jnp.where(core == 0, mine, other), jnp.where(core == 0, other, mine)
        blocks.append(jnp.concatenate([first, second], 0))
    split = [split3(b) for b in blocks]
    inner = tree_sum([gram6(s) for s in split]) * (1.0 / mode)
    inv = inverse_factor(inner)
    z, at = [], 0
    for s in range(n_row):
        start = 0
        for _ in range(counts[s]):
            x = pieces[at][...]
            hi, lo = split[s][0], split[s][1]
            if n_row == 4 and s in (1, 2):
                hi, lo = (jnp.where(core == 1, b, a) for a, b in zip((hi, lo), split[3 - s][:2]))
            stop = start + x.shape[0]
            z.append(mm3((hi[:, start:stop], lo[:, start:stop]), split2(x), NN))
            start, at = stop, at + 1
    z = tree_sum(z)
    rank_here = rank // n_row
    for i in range(n_row):
        rows_ref[i] = inv[i * rank_here : (i + 1) * rank_here]
    core_ref[...] = mm4(split2(rows_ref[row]), split2(z)) * (1.0 / math.sqrt(mode))
    inv2 = split2(inv)
    for s in range(n_row):
        block = mm4(inv2, split[s])
        if len(nf_ref.shape) == 3:
            nf_ref[row ^ s] = block
        else:
            nf_ref[:, pl.ds(pl.multiple_of((row ^ s) * rows_here, rows_here), rows_here)] = block


def gram_kernel(n_row, n_col, scale, counts, *refs):
    total = sum(counts)
    pieces, (given_ref, kept_ref, hi_ref, lo_ref, part_ref) = refs[:total], refs[total:]
    row = lax.axis_index("row")
    core = lax.axis_index("col") % 2
    n_z = n_col // 2
    rows_here = hi_ref.shape[1] * 2
    group = rows_here // 2
    half = group // n_col
    at = 0
    for s in range(n_row):
        hi, lo = [], []
        for _ in range(counts[s]):
            h, l = split2(pieces[at][...])
            hi.append(h)
            lo.append(l)
            at += 1
        hi, lo = jnp.concatenate(hi, 0), jnp.concatenate(lo, 0)
        owner = row ^ sided(s, n_row)
        for i in range(2):
            hi_ref[2 * owner + i] = hi[i * group : (i + 1) * group]
            lo_ref[2 * owner + i] = lo[i * group : (i + 1) * group]
    high = 2 * n_row - 1 - row
    left = (
        jnp.concatenate([hi_ref[high], hi_ref[row]], 0),
        jnp.concatenate([lo_ref[high], lo_ref[row]], 0),
    )
    for r in range(n_row):
        right = (
            jnp.concatenate([hi_ref[2 * r], hi_ref[2 * r + 1]], 0),
            jnp.concatenate([lo_ref[2 * r], lo_ref[2 * r + 1]], 0),
        )
        g = mm3(left, right, NT) * scale
        for i in range(2):
            for h in range(2):
                for p in range(n_col):
                    start = h * group + p * half
                    part_ref[h, 2 * r + i, p] = g[start : start + half, i * group : (i + 1) * group]
    n_high = 2 * n_row - row
    for b in range(2 * n_row + 1):
        is_low = (b >= n_high).astype(jnp.int32)
        block = b - is_low * n_high
        for zz in range(n_z):
            for ref, k in ((given_ref, 1 - core), (kept_ref, core)):
                owner = 2 * zz + k
                piece = jnp.where(is_low == 1, owner, n_col - 1 - owner)
                ref[zz, :, b * group : (b + 1) * group] = part_ref[is_low, block, piece]


def pieces_kernel(n_z, kept_ref, got_ref, keep_ref, give_ref):
    z = lax.axis_index("col") // 2
    for t in range(n_z):
        ref = give_ref if t % 2 else keep_ref
        at = z ^ sided(t, n_z)
        ref[t // 2] = kept_ref[at] + got_ref[at]


def unpack_kernel(n_row, n_col, *refs):
    out_ref = refs[-1]
    row = lax.axis_index("row")
    owner = row * n_col + lax.axis_index("col")
    total = tree_sum([r[0] for r in refs[:-1]])
    half, width = total.shape
    mode = out_ref.shape[1]
    group = width - mode
    r = lax.broadcasted_iota(jnp.int32, (half, mode), 0)
    c = lax.broadcasted_iota(jnp.int32, (half, mode), 1)
    out_ref[half:, :] = jnp.where(c <= mode - (owner + 1) * half + r, total[:, :mode], F32(0.0))
    out_ref[:half, :] = jnp.zeros((half, mode), F32)
    for k in range(n_row):

        @pl.when(row == k)
        def _():
            start, stop = mode - k * group, mode + group
            keep = c[:, : stop - start] <= owner * half + r[:, : stop - start]
            out_ref[:half, : stop - start] = jnp.where(keep, total[:, start:stop], F32(0.0))


def body(unfolding, factor):
    n_row = lax.axis_size("row")
    n_col = lax.axis_size("col")
    n_z = n_col // 2
    rows_here, cols_here = unfolding.shape
    mode = rows_here * n_row
    rank = factor.shape[1]
    hr = rank // 2
    scale = 1.0 / (cols_here * n_col)
    group = rows_here // 2
    half = group // n_col
    width = mode + group

    def over_row(x, s):
        return lax.ppermute(x, "row", [(i, i ^ s) for i in range(n_row)])

    def over_side(x, s):
        pairs = [((r, c), (r ^ (3 - s if c % 2 else s), c)) for r in range(n_row) for c in range(n_col)]
        return lax.ppermute(x, ("row", "col"), [(a * n_col + b, p * n_col + q) for (a, b), (p, q) in pairs])

    def over_col(x, s):
        return lax.ppermute(x, "col", [(i, i ^ s) for i in range(n_col)])

    def over_z(x, s):
        far = [2 * (3 - s if n_z == 4 and c % 2 else s) for c in range(n_col)]
        return lax.ppermute(x, "col", [(c, c ^ far[c]) for c in range(n_col)])

    def steps(n):
        return [1 << k for k in range(n.bit_length() - 1)]

    y_shape = jax.ShapeDtypeStruct((rank, cols_here), F32)
    part_shape = jax.ShapeDtypeStruct((group, cols_here), F32)
    project = functools.partial(project_kernel, rows_here)
    if n_row == 4:
        two_low = over_side(unfolding[group:], 2)
        y, upper, lower = call(
            project,
            (y_shape, part_shape, part_shape),
            factor.T,
            unfolding,
            work=COST["project"],
            name="project",
        )
        got = over_side(y, 1)
        one_up = over_side(upper, 1)
        one_low = over_side(lower, 1)
        y, upper = call(
            join_kernel, (y_shape, part_shape), y, got, upper, work=COST["join"], name="join"
        )
        y_got = over_side(y, 2)
        two_up = over_side(upper, 2)
        three = [over_side(one_up, 2), over_side(two_low, 1)]
        blocks = [[unfolding], [one_up, one_low], [two_up, two_low], three]
    else:
        (y,) = call(project, (y_shape,), factor.T, unfolding, work=COST["project"], name="project")
        for s in steps(n_row)[:-1]:
            y = y + over_row(y, s)
        y_got = over_row(y, n_row // 2)
        blocks = [[unfolding]] + [[over_row(unfolding, s)] for s in range(1, n_row)]
    counts = tuple(len(b) for b in blocks)
    blocks = [p for b in blocks for p in b]

    kept, given = call(
        functools.partial(term_kernel, scale),
        (jax.ShapeDtypeStruct((hr, rows_here), F32),) * 2,
        unfolding,
        y,
        y_got,
        work=COST["term"],
        name="term",
    )
    image = call(
        sum_kernel,
        jax.ShapeDtypeStruct((hr, rows_here), F32),
        kept,
        over_col(given, 1),
        work=COST["core_sum"],
        name="core_sum",
    )

    def z_sum(image, s, after):
        return call(
            sum_kernel,
            jax.ShapeDtypeStruct((hr, rows_here), F32),
            image,
            over_z(image, s),
            after=after,
            work=COST["sum"],
            name="z_sum",
        )

    for s in steps(n_z):
        image = z_sum(image, s, [])

    given, kept = call(
        functools.partial(gram_kernel, n_row, n_col, scale, counts),
        (jax.ShapeDtypeStruct((n_z, half, width), F32),) * 2,
        *blocks,
        scratch=[
            pltpu.VMEM((2 * n_row, group, cols_here), BF16),
            pltpu.VMEM((2 * n_row, group, cols_here), BF16),
            pltpu.VMEM((2, 2 * n_row, n_col, half, group), F32),
        ],
        after=[image],
        work=COST["gram"],
        name="gram",
    )
    mine = image[None]
    for s in steps(n_row):
        mine = call(
            stack_kernel,
            jax.ShapeDtypeStruct((2 * s, hr, rows_here), F32),
            mine,
            over_row(mine, s),
            after=[given] if s == 1 else [],
            work=COST["stack"],
            name="stack",
        )
    other = over_col(mine, 1)

    rank_here = rank // n_row
    whole = rows_here % 128 == 0
    nf, core_out = call(
        functools.partial(finish_kernel, n_row, counts),
        (
            jax.ShapeDtypeStruct((rank, mode) if whole else (n_row, rank, rows_here), F32),
            jax.ShapeDtypeStruct((rank_here, cols_here), F32),
        ),
        mine,
        other,
        *blocks,
        scratch=[pltpu.VMEM((n_row, rank_here, rank), F32)],
        work=COST["finish"],
        name="finish",
    )
    new_factor = nf.T if whole else nf.transpose(0, 2, 1).reshape(mode, rank)

    keep, give = call(
        functools.partial(pieces_kernel, n_z),
        (jax.ShapeDtypeStruct((n_z // 2, half, width), F32),) * 2,
        kept,
        over_col(given, 1),
        work=COST["pieces"],
        name="pieces",
    )
    got = over_z(give, 1)
    for s in steps(n_z)[1:]:
        keep, give = keep[0::2] + got[0::2], keep[1::2] + got[1::2]
        got = over_z(give, s)
    gram_lower = call(
        functools.partial(unpack_kernel, n_row, n_col),
        jax.ShapeDtypeStruct((2 * half, mode), F32),
        keep,
        got,
        work=COST["unpack"],
        name="unpack",
    )
    return gram_lower, new_factor, core_out


def solution(mesh):
    in_specs = (P("row", "col"), P())
    out_specs = (P(("row", "col"), None), P(), P("row", "col"))
    return jax.shard_map(body, mesh=mesh, in_specs=in_specs, out_specs=out_specs, check_vma=False)
```

profile of v0, /device:TPU:0, one launch (start us, length us, event | category | flops | bytes accessed | tf_op | source)
XLA Modules:
  0.0 45.7 jit_solution(11478169980266915205)
XLA Ops:
  0.6 1.0 %slice.19 = f32[128,512]{1,0:T(8,128)S(1)} slice(f32[256,512]{1,0:T(8,128)} %refs_2_.1), slice={[128:256], [0:512]} | slice | bytes 524288 | tf_op jit(solution)/shard_map/slice | solution.py:346
  1.7 3.0 %collective-permute-start.4 = (f32[128,512]{1,0:T(8,128)S(1)}, f32[128,512]{1,0:T(8,128)S(1)}, u32[]{:S(2)}, u32[]{:S(2)}) collective-permute-start(f32[128,512]{1,0:T(8,128)S(1)} %slice.19), channel_id=1, source_target_pairs={{0,16},{1,9},{2,18},{3,11},{4,20},{5,13},{6,22},{7,15},{8,24},{9,1... | collective-permute-start | bytes 786440 | tf_op jit(solution)/shard_map/ppermute | solution.py:330
  4.7 0.9 %copy-done.1 = f32[1024,64]{0,1:T(8,128)S(1)} copy-done((f32[1024,64]{0,1:T(8,128)S(1)}, f32[1024,64]{0,1:T(8,128)}, u32[]{:S(2)}) %copy-start.1) | copy-done | bytes 262168
  5.7 0.3 project.1
  5.9 1.6 %collective-permute-start.2 = (f32[64,512]{1,0:T(8,128)S(1)}, f32[64,512]{1,0:T(8,128)S(1)}, u32[]{:S(2)}, u32[]{:S(2)}) collective-permute-start(f32[64,512]{1,0:T(8,128)S(1)} %get-tuple-element.18.refs_0_), channel_id=1, source_target_pairs={{0,8},{1,17},{2,10},{3,19},{4,12},{5,21},{6,14},{7,23},{8,0},{9,25... | collective-permute-start | bytes 393224 | tf_op jit(solution)/shard_map/ppermute | solution.py:330
  7.5 0.5 %collective-permute-start = (f32[128,512]{1,0:T(8,128)S(1)}, f32[128,512]{1,0:T(8,128)S(1)}, u32[]{:S(2)}, u32[]{:S(2)}) collective-permute-start(f32[128,512]{1,0:T(8,128)S(1)} %get-tuple-element.16.refs_2_), channel_id=1, source_target_pairs={{0,8},{1,17},{2,10},{3,19},{4,12},{5,21},{6,14},{7,23},{8,0},{9,25... | collective-permute-start | bytes 786440 | tf_op jit(solution)/shard_map/ppermute | solution.py:330
  8.0 2.9 %collective-permute-done.2.refs_1_ = f32[64,512]{1,0:T(8,128)S(1)} collective-permute-done((f32[64,512]{1,0:T(8,128)S(1)}, f32[64,512]{1,0:T(8,128)S(1)}, u32[]{:S(2)}, u32[]{:S(2)}) %collective-permute-start.2) | collective-permute-done | bytes 131104 | tf_op jit(solution)/shard_map/ppermute | solution.py:330
  11.0 0.4 collective-permute-start.7
  11.4 1.6 %collective-permute-start.1 = (f32[128,512]{1,0:T(8,128)S(1)}, f32[128,512]{1,0:T(8,128)S(1)}, u32[]{:S(2)}, u32[]{:S(2)}) collective-permute-start(f32[128,512]{1,0:T(8,128)S(1)} %get-tuple-element.17), channel_id=1, source_target_pairs={{0,8},{1,17},{2,10},{3,19},{4,12},{5,21},{6,14},{7,23},{8,0},{9,25... | collective-permute-start | bytes 786440 | tf_op jit(solution)/shard_map/ppermute | solution.py:330
  13.1 1.5 %collective-permute-start.3 = (f32[128,512]{1,0:T(8,128)S(1)}, f32[128,512]{1,0:T(8,128)S(1)}, u32[]{:S(2)}, u32[]{:S(2)}) collective-permute-start(f32[128,512]{1,0:T(8,128)S(1)} %get-tuple-element.19), channel_id=1, source_target_pairs={{0,16},{1,9},{2,18},{3,11},{4,20},{5,13},{6,22},{7,15},{8,24},{9,1... | collective-permute-start | bytes 786440 | tf_op jit(solution)/shard_map/ppermute | solution.py:330
  14.6 0.5 %collective-permute-start.6 = (f32[128,512]{1,0:T(8,128)S(1)}, f32[128,512]{1,0:T(8,128)S(1)}, u32[]{:S(2)}, u32[]{:S(2)}) collective-permute-start(f32[128,512]{1,0:T(8,128)S(1)} %collective-permute-done.4.refs_4_.refs_6_), channel_id=1, source_target_pairs={{0,8},{1,17},{2,10},{3,19},{4,12},{5,21},{6,14},{7,23},{8,0},{9,25... | collective-permute-start | bytes 786440 | tf_op jit(solution)/shard_map/ppermute | solution.py:330
  15.1 0.4 collective-permute-start.5
  15.5 1.9 %collective-permute-done.7.refs_2_ = f32[64,512]{1,0:T(8,128)S(1)} collective-permute-done((f32[64,512]{1,0:T(8,128)S(1)}, f32[64,512]{1,0:T(8,128)S(1)}, u32[]{:S(2)}, u32[]{:S(2)}) %collective-permute-start.7) | collective-permute-done | bytes 131104 | tf_op jit(solution)/shard_map/ppermute | solution.py:330
  17.4 0.4 term.1
  17.8 0.1 collective-permute-start.8
  17.9 1.2 %collective-permute-done.8.refs_1_ = f32[32,256]{1,0:T(8,128)S(1)} collective-permute-done((f32[32,256]{1,0:T(8,128)S(1)}, f32[32,256]{1,0:T(8,128)S(1)}, u32[]{:S(2)}, u32[]{:S(2)}) %collective-permute-start.8) | collective-permute-done | bytes 32800 | tf_op jit(solution)/shard_map/ppermute | solution.py:333
  19.1 1.6 %collective-permute-start.9 = (f32[32,256]{1,0:T(8,128)S(1)}, f32[32,256]{1,0:T(8,128)S(1)}, u32[]{:S(2)}, u32[]{:S(2)}) collective-permute-start(f32[32,256]{1,0:T(8,128)S(1)} %core_sum.1.refs_0_), channel_id=1, source_target_pairs={{0,2},{1,5},{2,0},{3,7},{4,6},{5,1},{6,4},{7,3},{8,10},{9,13},{10,... | collective-permute-start | bytes 98312 | tf_op jit(solution)/shard_map/ppermute | solution.py:337
  20.6 2.7 %collective-permute-done.9.refs_1_ = f32[32,256]{1,0:T(8,128)S(1)} collective-permute-done((f32[32,256]{1,0:T(8,128)S(1)}, f32[32,256]{1,0:T(8,128)S(1)}, u32[]{:S(2)}, u32[]{:S(2)}) %collective-permute-start.9) | collective-permute-done | bytes 32800 | tf_op jit(solution)/shard_map/ppermute | solution.py:337
  23.3 2.2 %collective-permute-start.10 = (f32[32,256]{1,0:T(8,128)S(1)}, f32[32,256]{1,0:T(8,128)S(1)}, u32[]{:S(2)}, u32[]{:S(2)}) collective-permute-start(f32[32,256]{1,0:T(8,128)S(1)} %z_sum.2.refs_0_), channel_id=1, source_target_pairs={{0,4},{1,3},{2,6},{3,1},{4,0},{5,7},{6,2},{7,5},{8,12},{9,11},{10,... | collective-permute-start | bytes 98312 | tf_op jit(solution)/shard_map/ppermute | solution.py:337
  25.5 2.6 %collective-permute-done.10.refs_1_ = f32[32,256]{1,0:T(8,128)S(1)} collective-permute-done((f32[32,256]{1,0:T(8,128)S(1)}, f32[32,256]{1,0:T(8,128)S(1)}, u32[]{:S(2)}, u32[]{:S(2)}) %collective-permute-start.10) | collective-permute-done | bytes 32800 | tf_op jit(solution)/shard_map/ppermute | solution.py:337
  28.2 1.5 %collective-permute-start.14 = (f32[1,32,256]{2,1,0:T(8,128)S(1)}, f32[1,32,256]{2,1,0:T(8,128)S(1)}, u32[]{:S(2)}, u32[]{:S(2)}) collective-permute-start(f32[1,32,256]{2,1,0:T(8,128)S(1)} %bitcast.4), channel_id=1, source_target_pairs={{0,8},{8,0},{16,24},{24,16},{1,9},{9,1},{17,25},{25,17},{2,10},{10... | collective-permute-start | bytes 98312 | tf_op jit(solution)/shard_map/ppermute | solution.py:326
  29.7 1.6 %gram.1 = (f32[4,16,1152]{2,1,0:T(8,128)S(1)}, f32[4,16,1152]{2,1,0:T(8,128)S(1)}) custom-call(f32[256,512]{1,0:T(8,128)S(1)} %copy-done, f32[128,512]{1,0:T(8,128)S(1)} %collective-permute-done.refs_1_.refs_3_, f32[128,512]{1,0:T(8,128)S(1)} %collective-permute-done.1.refs_2_.refs_4_, f32[128,512]{1,0:T(8,128)S(1)} %collective-permute-done.3.refs_3_.refs_5_, ...), custom_call_target="tpu_custom_call" | custom-call | flops 1000000 | tf_op jit(solution)/shard_map/gram/pallas_call | solution.py:110
  31.3 0.8 %collective-permute-done.14.refs_1_ = f32[1,32,256]{2,1,0:T(8,128)S(1)} collective-permute-done((f32[1,32,256]{2,1,0:T(8,128)S(1)}, f32[1,32,256]{2,1,0:T(8,128)S(1)}, u32[]{:S(2)}, u32[]{:S(2)}) %collective-permute-start.14) | collective-permute-done | bytes 32800 | tf_op jit(solution)/shard_map/ppermute | solution.py:326
  32.1 0.5 %collective-permute-start.15 = (f32[2,32,256]{2,1,0:T(8,128)S(1)}, f32[2,32,256]{2,1,0:T(8,128)S(1)}, u32[]{:S(2)}, u32[]{:S(2)}) collective-permute-start(f32[2,32,256]{2,1,0:T(8,128)S(1)} %stack.2.refs_0_), channel_id=1, source_target_pairs={{0,16},{8,24},{16,0},{24,8},{1,17},{9,25},{17,1},{25,9},{2,18},{10... | collective-permute-start | bytes 196616 | tf_op jit(solution)/shard_map/ppermute | solution.py:326
  32.5 0.3 collective-permute-done.11.refs_1_
  32.9 1.4 %collective-permute-start.12 = (f32[2,16,1152]{2,1,0:T(8,128)S(1)}, f32[2,16,1152]{2,1,0:T(8,128)S(1)}, u32[]{:S(2)}, u32[]{:S(2)}) collective-permute-start(f32[2,16,1152]{2,1,0:T(8,128)S(1)} %get-tuple-element.26), channel_id=1, source_target_pairs={{0,2},{1,5},{2,0},{3,7},{4,6},{5,1},{6,4},{7,3},{8,10},{9,13},{10,... | collective-permute-start | bytes 442376 | tf_op jit(solution)/shard_map/ppermute | solution.py:337
  34.3 2.0 %collective-permute-done.15.refs_1_ = f32[2,32,256]{2,1,0:T(8,128)S(1)} collective-permute-done((f32[2,32,256]{2,1,0:T(8,128)S(1)}, f32[2,32,256]{2,1,0:T(8,128)S(1)}, u32[]{:S(2)}, u32[]{:S(2)}) %collective-permute-start.15) | collective-permute-done | bytes 65568 | tf_op jit(solution)/shard_map/ppermute | solution.py:326
  36.4 0.1 collective-permute-start.16
  36.4 3.3 %collective-permute-done.12 = f32[2,16,1152]{2,1,0:T(8,128)S(1)} collective-permute-done((f32[2,16,1152]{2,1,0:T(8,128)S(1)}, f32[2,16,1152]{2,1,0:T(8,128)S(1)}, u32[]{:S(2)}, u32[]{:S(2)}) %collective-permute-start.12) | collective-permute-done | bytes 147488 | tf_op jit(solution)/shard_map/ppermute | solution.py:337
  39.7 1.5 %collective-permute-start.13 = (f32[1,16,1152]{2,1,0:T(8,128)S(1)}, f32[1,16,1152]{2,1,0:T(8,128)S(1)}, u32[]{:S(2)}, u32[]{:S(2)}) collective-permute-start(f32[1,16,1152]{2,1,0:T(8,128)S(1)} %get-tuple-element.29), channel_id=1, source_target_pairs={{0,4},{1,3},{2,6},{3,1},{4,0},{5,7},{6,2},{7,5},{8,12},{9,11},{10,... | collective-permute-start | bytes 221192 | tf_op jit(solution)/shard_map/ppermute | solution.py:337
  41.2 3.8 %finish.1 = (f32[64,1024]{1,0:T(8,128)}, f32[16,512]{1,0:T(8,128)}) custom-call(f32[4,32,256]{2,1,0:T(8,128)S(1)} %stack.3.refs_0_, f32[4,32,256]{2,1,0:T(8,128)S(1)} %collective-permute-done.16.refs_1_, f32[256,512]{1,0:T(8,128)S(1)} %copy-done, f32[128,512]{1,0:T(8,128)S(1)} %collective-permute-done.refs_1_.refs_3_, ...), custom_call_target="tpu_custom_call" | custom-call | flops 10000000000 | tf_op jit(solution)/shard_map/finish/pallas_call | solution.py:110
  45.0 0.7 %unpack.1 = f32[32,1024]{1,0:T(8,128)} custom-call(f32[1,16,1152]{2,1,0:T(8,128)S(1)} %get-tuple-element.30.refs_0_, f32[1,16,1152]{2,1,0:T(8,128)S(1)} %collective-permute-done.13.refs_1_), custom_call_target="tpu_custom_call" | custom-call | flops 1000000 | tf_op jit(solution)/shard_map/unpack/pallas_call | solution.py:110
  (20 shorter events, 0.2 us)
Async XLA Ops:
  0.6 4.1 %copy-start = (f32[256,512]{1,0:T(8,128)S(1)}, f32[256,512]{1,0:T(8,128)}, u32[]{:S(2)}) copy-start(f32[256,512]{1,0:T(8,128)} %refs_2_.1) | copy-start | bytes 1572868
  1.7 12.9 %collective-permute-start.4 = (f32[128,512]{1,0:T(8,128)S(1)}, f32[128,512]{1,0:T(8,128)S(1)}, u32[]{:S(2)}, u32[]{:S(2)}) collective-permute-start(f32[128,512]{1,0:T(8,128)S(1)} %slice.19), channel_id=1, source_target_pairs={{0,16},{1,9},{2,18},{3,11},{4,20},{5,13},{6,22},{7,15},{8,24},{9,1... | collective-permute-start | bytes 786440 | tf_op jit(solution)/shard_map/ppermute | solution.py:330
  4.7 1.0 %copy-start.1 = (f32[1024,64]{0,1:T(8,128)S(1)}, f32[1024,64]{0,1:T(8,128)}, u32[]{:S(2)}) copy-start(f32[1024,64]{0,1:T(8,128)} %param.3) | copy-start | bytes 786436
  5.9 5.0 %collective-permute-start.2 = (f32[64,512]{1,0:T(8,128)S(1)}, f32[64,512]{1,0:T(8,128)S(1)}, u32[]{:S(2)}, u32[]{:S(2)}) collective-permute-start(f32[64,512]{1,0:T(8,128)S(1)} %get-tuple-element.18.refs_0_), channel_id=1, source_target_pairs={{0,8},{1,17},{2,10},{3,19},{4,12},{5,21},{6,14},{7,23},{8,0},{9,25... | collective-permute-start | bytes 393224 | tf_op jit(solution)/shard_map/ppermute | solution.py:330
  7.5 7.6 %collective-permute-start = (f32[128,512]{1,0:T(8,128)S(1)}, f32[128,512]{1,0:T(8,128)S(1)}, u32[]{:S(2)}, u32[]{:S(2)}) collective-permute-start(f32[128,512]{1,0:T(8,128)S(1)} %get-tuple-element.16.refs_2_), channel_id=1, source_target_pairs={{0,8},{1,17},{2,10},{3,19},{4,12},{5,21},{6,14},{7,23},{8,0},{9,25... | collective-permute-start | bytes 786440 | tf_op jit(solution)/shard_map/ppermute | solution.py:330
  11.0 6.4 %collective-permute-start.7 = (f32[64,512]{1,0:T(8,128)S(1)}, f32[64,512]{1,0:T(8,128)S(1)}, u32[]{:S(2)}, u32[]{:S(2)}) collective-permute-start(f32[64,512]{1,0:T(8,128)S(1)} %get-tuple-element.20.refs_1_), channel_id=1, source_target_pairs={{0,16},{1,9},{2,18},{3,11},{4,20},{5,13},{6,22},{7,15},{8,24},{9,1... | collective-permute-start | bytes 393224 | tf_op jit(solution)/shard_map/ppermute | solution.py:330
  11.4 18.2 %collective-permute-start.1 = (f32[128,512]{1,0:T(8,128)S(1)}, f32[128,512]{1,0:T(8,128)S(1)}, u32[]{:S(2)}, u32[]{:S(2)}) collective-permute-start(f32[128,512]{1,0:T(8,128)S(1)} %get-tuple-element.17), channel_id=1, source_target_pairs={{0,8},{1,17},{2,10},{3,19},{4,12},{5,21},{6,14},{7,23},{8,0},{9,25... | collective-permute-start | bytes 786440 | tf_op jit(solution)/shard_map/ppermute | solution.py:330
  13.1 16.6 %collective-permute-start.3 = (f32[128,512]{1,0:T(8,128)S(1)}, f32[128,512]{1,0:T(8,128)S(1)}, u32[]{:S(2)}, u32[]{:S(2)}) collective-permute-start(f32[128,512]{1,0:T(8,128)S(1)} %get-tuple-element.19), channel_id=1, source_target_pairs={{0,16},{1,9},{2,18},{3,11},{4,20},{5,13},{6,22},{7,15},{8,24},{9,1... | collective-permute-start | bytes 786440 | tf_op jit(solution)/shard_map/ppermute | solution.py:330
  14.6 15.1 %collective-permute-start.6 = (f32[128,512]{1,0:T(8,128)S(1)}, f32[128,512]{1,0:T(8,128)S(1)}, u32[]{:S(2)}, u32[]{:S(2)}) collective-permute-start(f32[128,512]{1,0:T(8,128)S(1)} %collective-permute-done.4.refs_4_.refs_6_), channel_id=1, source_target_pairs={{0,8},{1,17},{2,10},{3,19},{4,12},{5,21},{6,14},{7,23},{8,0},{9,25... | collective-permute-start | bytes 786440 | tf_op jit(solution)/shard_map/ppermute | solution.py:330
  15.1 14.5 %collective-permute-start.5 = (f32[128,512]{1,0:T(8,128)S(1)}, f32[128,512]{1,0:T(8,128)S(1)}, u32[]{:S(2)}, u32[]{:S(2)}) collective-permute-start(f32[128,512]{1,0:T(8,128)S(1)} %collective-permute-done.refs_1_.refs_3_), channel_id=1, source_target_pairs={{0,16},{1,9},{2,18},{3,11},{4,20},{5,13},{6,22},{7,15},{8,24},{9,1... | collective-permute-start | bytes 786440 | tf_op jit(solution)/shard_map/ppermute | solution.py:330
  17.8 1.3 %collective-permute-start.8 = (f32[32,256]{1,0:T(8,128)S(1)}, f32[32,256]{1,0:T(8,128)S(1)}, u32[]{:S(2)}, u32[]{:S(2)}) collective-permute-start(f32[32,256]{1,0:T(8,128)S(1)} %get-tuple-element.22), channel_id=1, source_target_pairs={{0,1},{1,0},{2,3},{3,2},{4,5},{5,4},{6,7},{7,6},{8,9},{9,8},{10,11... | collective-permute-start | bytes 98312 | tf_op jit(solution)/shard_map/ppermute | solution.py:333
  19.1 4.3 %collective-permute-start.9 = (f32[32,256]{1,0:T(8,128)S(1)}, f32[32,256]{1,0:T(8,128)S(1)}, u32[]{:S(2)}, u32[]{:S(2)}) collective-permute-start(f32[32,256]{1,0:T(8,128)S(1)} %core_sum.1.refs_0_), channel_id=1, source_target_pairs={{0,2},{1,5},{2,0},{3,7},{4,6},{5,1},{6,4},{7,3},{8,10},{9,13},{10,... | collective-permute-start | bytes 98312 | tf_op jit(solution)/shard_map/ppermute | solution.py:337
  23.3 4.8 %collective-permute-start.10 = (f32[32,256]{1,0:T(8,128)S(1)}, f32[32,256]{1,0:T(8,128)S(1)}, u32[]{:S(2)}, u32[]{:S(2)}) collective-permute-start(f32[32,256]{1,0:T(8,128)S(1)} %z_sum.2.refs_0_), channel_id=1, source_target_pairs={{0,4},{1,3},{2,6},{3,1},{4,0},{5,7},{6,2},{7,5},{8,12},{9,11},{10,... | collective-permute-start | bytes 98312 | tf_op jit(solution)/shard_map/ppermute | solution.py:337
  28.2 3.9 %collective-permute-start.14 = (f32[1,32,256]{2,1,0:T(8,128)S(1)}, f32[1,32,256]{2,1,0:T(8,128)S(1)}, u32[]{:S(2)}, u32[]{:S(2)}) collective-permute-start(f32[1,32,256]{2,1,0:T(8,128)S(1)} %bitcast.4), channel_id=1, source_target_pairs={{0,8},{8,0},{16,24},{24,16},{1,9},{9,1},{17,25},{25,17},{2,10},{10... | collective-permute-start | bytes 98312 | tf_op jit(solution)/shard_map/ppermute | solution.py:326
  31.2 1.6 %collective-permute-start.11 = (f32[4,16,1152]{2,1,0:T(8,128)S(1)}, f32[4,16,1152]{2,1,0:T(8,128)S(1)}, u32[]{:S(2)}, u32[]{:S(2)}) collective-permute-start(f32[4,16,1152]{2,1,0:T(8,128)S(1)} %get-tuple-element.24.refs_2_), channel_id=1, source_target_pairs={{0,1},{1,0},{2,3},{3,2},{4,5},{5,4},{6,7},{7,6},{8,9},{9,8},{10,11... | collective-permute-start | bytes 884744 | tf_op jit(solution)/shard_map/ppermute | solution.py:333
  32.1 4.3 %collective-permute-start.15 = (f32[2,32,256]{2,1,0:T(8,128)S(1)}, f32[2,32,256]{2,1,0:T(8,128)S(1)}, u32[]{:S(2)}, u32[]{:S(2)}) collective-permute-start(f32[2,32,256]{2,1,0:T(8,128)S(1)} %stack.2.refs_0_), channel_id=1, source_target_pairs={{0,16},{8,24},{16,0},{24,8},{1,17},{9,25},{17,1},{25,9},{2,18},{10... | collective-permute-start | bytes 196616 | tf_op jit(solution)/shard_map/ppermute | solution.py:326
  32.9 6.8 %collective-permute-start.12 = (f32[2,16,1152]{2,1,0:T(8,128)S(1)}, f32[2,16,1152]{2,1,0:T(8,128)S(1)}, u32[]{:S(2)}, u32[]{:S(2)}) collective-permute-start(f32[2,16,1152]{2,1,0:T(8,128)S(1)} %get-tuple-element.26), channel_id=1, source_target_pairs={{0,2},{1,5},{2,0},{3,7},{4,6},{5,1},{6,4},{7,3},{8,10},{9,13},{10,... | collective-permute-start | bytes 442376 | tf_op jit(solution)/shard_map/ppermute | solution.py:337
  36.4 4.9 %collective-permute-start.16 = (f32[4,32,256]{2,1,0:T(8,128)S(1)}, f32[4,32,256]{2,1,0:T(8,128)S(1)}, u32[]{:S(2)}, u32[]{:S(2)}) collective-permute-start(f32[4,32,256]{2,1,0:T(8,128)S(1)} %stack.3.refs_0_), channel_id=1, source_target_pairs={{0,1},{1,0},{2,3},{3,2},{4,5},{5,4},{6,7},{7,6},{8,9},{9,8},{10,11... | collective-permute-start | bytes 393224 | tf_op jit(solution)/shard_map/ppermute | solution.py:333
  39.7 5.3 %collective-permute-start.13 = (f32[1,16,1152]{2,1,0:T(8,128)S(1)}, f32[1,16,1152]{2,1,0:T(8,128)S(1)}, u32[]{:S(2)}, u32[]{:S(2)}) collective-permute-start(f32[1,16,1152]{2,1,0:T(8,128)S(1)} %get-tuple-element.29), channel_id=1, source_target_pairs={{0,4},{1,3},{2,6},{3,1},{4,0},{5,7},{6,2},{7,5},{8,12},{9,11},{10,... | collective-permute-start | bytes 221192 | tf_op jit(solution)/shard_map/ppermute | solution.py:337
where the time goes:
time: 45.9 us; the launch traced here: 45.7 us
  starting transfers between devices  18.5 us (40%)
  waiting for transfers between devices  17.7 us (39%)
  Pallas kernels  6.75 us (15%)
  local copies, waits for them, and re-layouts  1.99 us (4%)
  between operations  0.73 us (2%)
    ppermute x8, starting transfers between devices, over_side(): lax.ppermute(x, ('row', 'col'), [(a * n_col + b, p * n_col + q) for (a, b...  9.62 us
    ppermute x4, waiting for transfers between devices, over_z(): return lax.ppermute(x, 'col', [(c, c ^ far[c]) for c in range(n_col)])  8.57 us
    pallas_call x12, Pallas kernels, call(): pl.pallas_call(run, out_shape=out_shape, in_specs=[pl.BlockSpec(memory_sp...  6.75 us
    ppermute x4, starting transfers between devices, over_z(): return lax.ppermute(x, 'col', [(c, c ^ far[c]) for c in range(n_col)])  6.72 us
    ppermute x8, waiting for transfers between devices, over_side(): lax.ppermute(x, ('row', 'col'), [(a * n_col + b, p * n_col + q) for (a, b...  4.86 us
    ppermute x2, waiting for transfers between devices, over_row(): return lax.ppermute(x, 'row', [(i, i ^ s) for i in range(n_row)])  2.78 us
    ppermute x2, starting transfers between devices, over_row(): return lax.ppermute(x, 'row', [(i, i ^ s) for i in range(n_row)])  1.96 us
    ppermute x3, waiting for transfers between devices, over_col(): return lax.ppermute(x, 'col', [(i, i ^ s) for i in range(n_col)])  1.52 us
  transfers between devices with their start and end apart: 17, of which 9 were waited for; matrix products, arithmetic and copies ran while one was open for 0% of the time, Pallas kernels for 13%

commit v1 on v0

--- a/solution.py
+++ b/solution.py
@@ -389,19 +389,19 @@
         name="core_sum",
     )
 
-    def z_sum(image, s, after):
+    def z_sum(image, s, after, work):
         return call(
             sum_kernel,
             jax.ShapeDtypeStruct((hr, rows_here), F32),
             image,
             over_z(image, s),
             after=after,
-            work=COST["sum"],
+            work=work,
             name="z_sum",
         )
 
-    for s in steps(n_z):
-        image = z_sum(image, s, [])
+    for s in steps(n_z)[:-1]:
+        image = z_sum(image, s, [], COST["sum"])
 
     given, kept = call(
         functools.partial(gram_kernel, n_row, n_col, scale, counts),
@@ -416,6 +416,7 @@
         work=COST["gram"],
         name="gram",
     )
+    image = z_sum(image, n_z // 2, [given], COST["stack"])
     mine = image[None]
     for s in steps(n_row):
         mine = call(
@@ -423,7 +424,6 @@
             jax.ShapeDtypeStruct((2 * s, hr, rows_here), F32),
             mine,
             over_row(mine, s),
-            after=[given] if s == 1 else [],
             work=COST["stack"],
             name="stack",
         )

time: 45.9 us -> 46.7 us (1.017)
  starting transfers between devices: 18.5 us -> 20.9 us
  waiting for transfers between devices: 17.7 us -> 16.2 us
    ppermute x4, waiting for transfers between devices: 8.57 us -> 5.68 us  [over_z(): return lax.ppermute(x, 'col', [(c, c ^ far[c]) for c in range(n_col)])]
    ppermute x4, starting transfers between devices: 6.72 us -> 8.18 us  [over_z(): return lax.ppermute(x, 'col', [(c, c ^ far[c]) for c in range(n_col)])]
    ppermute x2, starting transfers between devices: 1.96 us -> 2.92 us  [over_row(): return lax.ppermute(x, 'row', [(i, i ^ s) for i in range(n_row)])]
    ppermute x8, waiting for transfers between devices: 4.86 us -> 5.71 us  [over_side(): lax.ppermute(x, ('row', 'col'), [(a * n_col + b, p * n_col + q) for (a, b...]
    ppermute x2, waiting for transfers between devices: 2.78 us -> 3.58 us  [over_row(): return lax.ppermute(x, 'row', [(i, i ^ s) for i in range(n_row)])]
  transfers between devices with their start and end apart: 17 -> 17, of which waited for: 9 -> 10; matrix products, arithmetic and copies ran while one was open for 0% -> 0% of each run, Pallas kernels for 13% -> 13%
where the time goes in v1:
time: 46.7 us; the launch traced here: 46.5 us
  starting transfers between devices  20.9 us (45%)
  waiting for transfers between devices  16.2 us (35%)
  Pallas kernels  6.75 us (14%)
  local copies, waits for them, and re-layouts  1.99 us (4%)
  between operations  0.71 us (2%)
    ppermute x8, starting transfers between devices, over_side(): lax.ppermute(x, ('row', 'col'), [(a * n_col + b, p * n_col + q) for (a, b...  9.62 us
    ppermute x4, starting transfers between devices, over_z(): return lax.ppermute(x, 'col', [(c, c ^ far[c]) for c in range(n_col)])  8.18 us
    pallas_call x12, Pallas kernels, call(): pl.pallas_call(run, out_shape=out_shape, in_specs=[pl.BlockSpec(memory_sp...  6.75 us
    ppermute x8, waiting for transfers between devices, over_side(): lax.ppermute(x, ('row', 'col'), [(a * n_col + b, p * n_col + q) for (a, b...  5.71 us
    ppermute x4, waiting for transfers between devices, over_z(): return lax.ppermute(x, 'col', [(c, c ^ far[c]) for c in range(n_col)])  5.68 us
    ppermute x2, waiting for transfers between devices, over_row(): return lax.ppermute(x, 'row', [(i, i ^ s) for i in range(n_row)])  3.58 us
    ppermute x2, starting transfers between devices, over_row(): return lax.ppermute(x, 'row', [(i, i ^ s) for i in range(n_row)])  2.92 us
    ppermute x3, waiting for transfers between devices, over_col(): return lax.ppermute(x, 'col', [(i, i ^ s) for i in range(n_col)])  1.2 us
  transfers between devices with their start and end apart: 17, of which 10 were waited for; matrix products, arithmetic and copies ran while one was open for 0% of the time, Pallas kernels for 13%

profile of v1, /device:TPU:0, one launch (start us, length us, event | category | flops | bytes accessed | tf_op | source)
XLA Modules:
  0.0 46.5 jit_solution(6815364204571684548)
XLA Ops:
  0.6 1.0 %slice.19 = f32[128,512]{1,0:T(8,128)S(1)} slice(f32[256,512]{1,0:T(8,128)} %refs_2_.1), slice={[128:256], [0:512]} | slice | bytes 524288 | tf_op jit(solution)/shard_map/slice | solution.py:346
  1.7 3.0 %collective-permute-start.4 = (f32[128,512]{1,0:T(8,128)S(1)}, f32[128,512]{1,0:T(8,128)S(1)}, u32[]{:S(2)}, u32[]{:S(2)}) collective-permute-start(f32[128,512]{1,0:T(8,128)S(1)} %slice.19), channel_id=1, source_target_pairs={{0,16},{1,9},{2,18},{3,11},{4,20},{5,13},{6,22},{7,15},{8,24},{9,1... | collective-permute-start | bytes 786440 | tf_op jit(solution)/shard_map/ppermute | solution.py:330
  4.7 0.9 %copy-done.1 = f32[1024,64]{0,1:T(8,128)S(1)} copy-done((f32[1024,64]{0,1:T(8,128)S(1)}, f32[1024,64]{0,1:T(8,128)}, u32[]{:S(2)}) %copy-start.1) | copy-done | bytes 262168
  5.7 0.3 project.1
  5.9 1.6 %collective-permute-start.2 = (f32[64,512]{1,0:T(8,128)S(1)}, f32[64,512]{1,0:T(8,128)S(1)}, u32[]{:S(2)}, u32[]{:S(2)}) collective-permute-start(f32[64,512]{1,0:T(8,128)S(1)} %get-tuple-element.18.refs_0_), channel_id=1, source_target_pairs={{0,8},{1,17},{2,10},{3,19},{4,12},{5,21},{6,14},{7,23},{8,0},{9,25... | collective-permute-start | bytes 393224 | tf_op jit(solution)/shard_map/ppermute | solution.py:330
  7.5 0.5 %collective-permute-start = (f32[128,512]{1,0:T(8,128)S(1)}, f32[128,512]{1,0:T(8,128)S(1)}, u32[]{:S(2)}, u32[]{:S(2)}) collective-permute-start(f32[128,512]{1,0:T(8,128)S(1)} %get-tuple-element.16.refs_2_), channel_id=1, source_target_pairs={{0,8},{1,17},{2,10},{3,19},{4,12},{5,21},{6,14},{7,23},{8,0},{9,25... | collective-permute-start | bytes 786440 | tf_op jit(solution)/shard_map/ppermute | solution.py:330
  8.0 2.9 %collective-permute-done.2.refs_1_ = f32[64,512]{1,0:T(8,128)S(1)} collective-permute-done((f32[64,512]{1,0:T(8,128)S(1)}, f32[64,512]{1,0:T(8,128)S(1)}, u32[]{:S(2)}, u32[]{:S(2)}) %collective-permute-start.2) | collective-permute-done | bytes 131104 | tf_op jit(solution)/shard_map/ppermute | solution.py:330
  11.0 0.4 collective-permute-start.7
  11.4 1.6 %collective-permute-start.1 = (f32[128,512]{1,0:T(8,128)S(1)}, f32[128,512]{1,0:T(8,128)S(1)}, u32[]{:S(2)}, u32[]{:S(2)}) collective-permute-start(f32[128,512]{1,0:T(8,128)S(1)} %get-tuple-element.17), channel_id=1, source_target_pairs={{0,8},{1,17},{2,10},{3,19},{4,12},{5,21},{6,14},{7,23},{8,0},{9,25... | collective-permute-start | bytes 786440 | tf_op jit(solution)/shard_map/ppermute | solution.py:330
  13.1 1.5 %collective-permute-start.3 = (f32[128,512]{1,0:T(8,128)S(1)}, f32[128,512]{1,0:T(8,128)S(1)}, u32[]{:S(2)}, u32[]{:S(2)}) collective-permute-start(f32[128,512]{1,0:T(8,128)S(1)} %get-tuple-element.19), channel_id=1, source_target_pairs={{0,16},{1,9},{2,18},{3,11},{4,20},{5,13},{6,22},{7,15},{8,24},{9,1... | collective-permute-start | bytes 786440 | tf_op jit(solution)/shard_map/ppermute | solution.py:330
  14.6 0.5 %collective-permute-start.6 = (f32[128,512]{1,0:T(8,128)S(1)}, f32[128,512]{1,0:T(8,128)S(1)}, u32[]{:S(2)}, u32[]{:S(2)}) collective-permute-start(f32[128,512]{1,0:T(8,128)S(1)} %collective-permute-done.4.refs_4_.refs_6_), channel_id=1, source_target_pairs={{0,8},{1,17},{2,10},{3,19},{4,12},{5,21},{6,14},{7,23},{8,0},{9,25... | collective-permute-start | bytes 786440 | tf_op jit(solution)/shard_map/ppermute | solution.py:330
  15.1 0.4 collective-permute-start.5
  15.5 1.9 %collective-permute-done.7.refs_2_ = f32[64,512]{1,0:T(8,128)S(1)} collective-permute-done((f32[64,512]{1,0:T(8,128)S(1)}, f32[64,512]{1,0:T(8,128)S(1)}, u32[]{:S(2)}, u32[]{:S(2)}) %collective-permute-start.7) | collective-permute-done | bytes 131104 | tf_op jit(solution)/shard_map/ppermute | solution.py:330
  17.4 0.4 term.1
  17.8 0.1 collective-permute-start.8
  17.9 1.2 %collective-permute-done.8.refs_1_ = f32[32,256]{1,0:T(8,128)S(1)} collective-permute-done((f32[32,256]{1,0:T(8,128)S(1)}, f32[32,256]{1,0:T(8,128)S(1)}, u32[]{:S(2)}, u32[]{:S(2)}) %collective-permute-start.8) | collective-permute-done | bytes 32800 | tf_op jit(solution)/shard_map/ppermute | solution.py:333
  19.1 1.6 %collective-permute-start.9 = (f32[32,256]{1,0:T(8,128)S(1)}, f32[32,256]{1,0:T(8,128)S(1)}, u32[]{:S(2)}, u32[]{:S(2)}) collective-permute-start(f32[32,256]{1,0:T(8,128)S(1)} %core_sum.1.refs_0_), channel_id=1, source_target_pairs={{0,2},{1,5},{2,0},{3,7},{4,6},{5,1},{6,4},{7,3},{8,10},{9,13},{10,... | collective-permute-start | bytes 98312 | tf_op jit(solution)/shard_map/ppermute | solution.py:337
  20.6 2.7 %collective-permute-done.9.refs_1_ = f32[32,256]{1,0:T(8,128)S(1)} collective-permute-done((f32[32,256]{1,0:T(8,128)S(1)}, f32[32,256]{1,0:T(8,128)S(1)}, u32[]{:S(2)}, u32[]{:S(2)}) %collective-permute-start.9) | collective-permute-done | bytes 32800 | tf_op jit(solution)/shard_map/ppermute | solution.py:337
  23.3 2.2 %collective-permute-start.13 = (f32[32,256]{1,0:T(8,128)S(1)}, f32[32,256]{1,0:T(8,128)S(1)}, u32[]{:S(2)}, u32[]{:S(2)}) collective-permute-start(f32[32,256]{1,0:T(8,128)S(1)} %z_sum.2.refs_7_.refs_0_), channel_id=1, source_target_pairs={{0,4},{1,3},{2,6},{3,1},{4,0},{5,7},{6,2},{7,5},{8,12},{9,11},{10,... | collective-permute-start | bytes 98312 | tf_op jit(solution)/shard_map/ppermute | solution.py:337
  25.6 0.8 %collective-permute-done.6.refs_6_.refs_8_ = f32[128,512]{1,0:T(8,128)S(1)} collective-permute-done((f32[128,512]{1,0:T(8,128)S(1)}, f32[128,512]{1,0:T(8,128)S(1)}, u32[]{:S(2)}, u32[]{:S(2)}) %collective-permute-start.6) | collective-permute-done | bytes 262176 | tf_op jit(solution)/shard_map/ppermute | solution.py:330
  26.3 0.1 collective-permute-done.5.refs_5_.refs_7_
  26.4 1.5 %gram.1 = (f32[4,16,1152]{2,1,0:T(8,128)S(1)}, f32[4,16,1152]{2,1,0:T(8,128)S(1)}) custom-call(f32[256,512]{1,0:T(8,128)S(1)} %copy-done, f32[128,512]{1,0:T(8,128)S(1)} %collective-permute-done.refs_1_.refs_3_, f32[128,512]{1,0:T(8,128)S(1)} %collective-permute-done.1.refs_2_.refs_4_, f32[128,512]{1,0:T(8,128)S(1)} %collective-permute-done.3.refs_3_.refs_5_, ...), custom_call_target="tpu_custom_call" | custom-call | flops 1000000 | tf_op jit(solution)/shard_map/gram/pallas_call | solution.py:110
  28.0 0.2 collective-permute-done.13.refs_1_
  28.2 1.5 %collective-permute-start.14 = (f32[1,32,256]{2,1,0:T(8,128)S(1)}, f32[1,32,256]{2,1,0:T(8,128)S(1)}, u32[]{:S(2)}, u32[]{:S(2)}) collective-permute-start(f32[1,32,256]{2,1,0:T(8,128)S(1)} %bitcast.4), channel_id=1, source_target_pairs={{0,8},{8,0},{16,24},{24,16},{1,9},{9,1},{17,25},{25,17},{2,10},{10... | collective-permute-start | bytes 98312 | tf_op jit(solution)/shard_map/ppermute | solution.py:326
  29.6 2.4 %collective-permute-done.14.refs_1_ = f32[1,32,256]{2,1,0:T(8,128)S(1)} collective-permute-done((f32[1,32,256]{2,1,0:T(8,128)S(1)}, f32[1,32,256]{2,1,0:T(8,128)S(1)}, u32[]{:S(2)}, u32[]{:S(2)}) %collective-permute-start.14) | collective-permute-done | bytes 32800 | tf_op jit(solution)/shard_map/ppermute | solution.py:326
  32.1 1.4 %collective-permute-start.15 = (f32[2,32,256]{2,1,0:T(8,128)S(1)}, f32[2,32,256]{2,1,0:T(8,128)S(1)}, u32[]{:S(2)}, u32[]{:S(2)}) collective-permute-start(f32[2,32,256]{2,1,0:T(8,128)S(1)} %stack.2.refs_0_), channel_id=1, source_target_pairs={{0,16},{8,24},{16,0},{24,8},{1,17},{9,25},{17,1},{25,9},{2,18},{10... | collective-permute-start | bytes 196616 | tf_op jit(solution)/shard_map/ppermute | solution.py:326
  33.5 1.6 %collective-permute-start.11 = (f32[2,16,1152]{2,1,0:T(8,128)S(1)}, f32[2,16,1152]{2,1,0:T(8,128)S(1)}, u32[]{:S(2)}, u32[]{:S(2)}) collective-permute-start(f32[2,16,1152]{2,1,0:T(8,128)S(1)} %get-tuple-element.26), channel_id=1, source_target_pairs={{0,2},{1,5},{2,0},{3,7},{4,6},{5,1},{6,4},{7,3},{8,10},{9,13},{10,... | collective-permute-start | bytes 442376 | tf_op jit(solution)/shard_map/ppermute | solution.py:337
  35.2 1.1 %collective-permute-done.15.refs_1_ = f32[2,32,256]{2,1,0:T(8,128)S(1)} collective-permute-done((f32[2,32,256]{2,1,0:T(8,128)S(1)}, f32[2,32,256]{2,1,0:T(8,128)S(1)}, u32[]{:S(2)}, u32[]{:S(2)}) %collective-permute-start.15) | collective-permute-done | bytes 65568 | tf_op jit(solution)/shard_map/ppermute | solution.py:326
  36.4 2.8 %collective-permute-done.11 = f32[2,16,1152]{2,1,0:T(8,128)S(1)} collective-permute-done((f32[2,16,1152]{2,1,0:T(8,128)S(1)}, f32[2,16,1152]{2,1,0:T(8,128)S(1)}, u32[]{:S(2)}, u32[]{:S(2)}) %collective-permute-start.11) | collective-permute-done | bytes 147488 | tf_op jit(solution)/shard_map/ppermute | solution.py:337
  39.2 2.8 %collective-permute-start.12 = (f32[1,16,1152]{2,1,0:T(8,128)S(1)}, f32[1,16,1152]{2,1,0:T(8,128)S(1)}, u32[]{:S(2)}, u32[]{:S(2)}) collective-permute-start(f32[1,16,1152]{2,1,0:T(8,128)S(1)} %get-tuple-element.29), channel_id=1, source_target_pairs={{0,4},{1,3},{2,6},{3,1},{4,0},{5,7},{6,2},{7,5},{8,12},{9,11},{10,... | collective-permute-start | bytes 221192 | tf_op jit(solution)/shard_map/ppermute | solution.py:337
  42.0 3.8 %finish.1 = (f32[64,1024]{1,0:T(8,128)}, f32[16,512]{1,0:T(8,128)}) custom-call(f32[4,32,256]{2,1,0:T(8,128)S(1)} %stack.3.refs_0_, f32[4,32,256]{2,1,0:T(8,128)S(1)} %collective-permute-done.16.refs_1_, f32[256,512]{1,0:T(8,128)S(1)} %copy-done, f32[128,512]{1,0:T(8,128)S(1)} %collective-permute-done.refs_1_.refs_3_, ...), custom_call_target="tpu_custom_call" | custom-call | flops 10000000000 | tf_op jit(solution)/shard_map/finish/pallas_call | solution.py:110
  45.8 0.7 %unpack.1 = f32[32,1024]{1,0:T(8,128)} custom-call(f32[1,16,1152]{2,1,0:T(8,128)S(1)} %get-tuple-element.30.refs_0_, f32[1,16,1152]{2,1,0:T(8,128)S(1)} %collective-permute-done.12.refs_1_), custom_call_target="tpu_custom_call" | custom-call | flops 1000000 | tf_op jit(solution)/shard_map/unpack/pallas_call | solution.py:110
  (20 shorter events, 0.2 us)
Async XLA Ops:
  0.6 4.1 %copy-start = (f32[256,512]{1,0:T(8,128)S(1)}, f32[256,512]{1,0:T(8,128)}, u32[]{:S(2)}) copy-start(f32[256,512]{1,0:T(8,128)} %refs_2_.1) | copy-start | bytes 1572868
  1.7 12.9 %collective-permute-start.4 = (f32[128,512]{1,0:T(8,128)S(1)}, f32[128,512]{1,0:T(8,128)S(1)}, u32[]{:S(2)}, u32[]{:S(2)}) collective-permute-start(f32[128,512]{1,0:T(8,128)S(1)} %slice.19), channel_id=1, source_target_pairs={{0,16},{1,9},{2,18},{3,11},{4,20},{5,13},{6,22},{7,15},{8,24},{9,1... | collective-permute-start | bytes 786440 | tf_op jit(solution)/shard_map/ppermute | solution.py:330
  4.7 1.0 %copy-start.1 = (f32[1024,64]{0,1:T(8,128)S(1)}, f32[1024,64]{0,1:T(8,128)}, u32[]{:S(2)}) copy-start(f32[1024,64]{0,1:T(8,128)} %param.3) | copy-start | bytes 786436
  5.9 5.0 %collective-permute-start.2 = (f32[64,512]{1,0:T(8,128)S(1)}, f32[64,512]{1,0:T(8,128)S(1)}, u32[]{:S(2)}, u32[]{:S(2)}) collective-permute-start(f32[64,512]{1,0:T(8,128)S(1)} %get-tuple-element.18.refs_0_), channel_id=1, source_target_pairs={{0,8},{1,17},{2,10},{3,19},{4,12},{5,21},{6,14},{7,23},{8,0},{9,25... | collective-permute-start | bytes 393224 | tf_op jit(solution)/shard_map/ppermute | solution.py:330
  7.5 7.6 %collective-permute-start = (f32[128,512]{1,0:T(8,128)S(1)}, f32[128,512]{1,0:T(8,128)S(1)}, u32[]{:S(2)}, u32[]{:S(2)}) collective-permute-start(f32[128,512]{1,0:T(8,128)S(1)} %get-tuple-element.16.refs_2_), channel_id=1, source_target_pairs={{0,8},{1,17},{2,10},{3,19},{4,12},{5,21},{6,14},{7,23},{8,0},{9,25... | collective-permute-start | bytes 786440 | tf_op jit(solution)/shard_map/ppermute | solution.py:330
  11.0 6.4 %collective-permute-start.7 = (f32[64,512]{1,0:T(8,128)S(1)}, f32[64,512]{1,0:T(8,128)S(1)}, u32[]{:S(2)}, u32[]{:S(2)}) collective-permute-start(f32[64,512]{1,0:T(8,128)S(1)} %get-tuple-element.20.refs_1_), channel_id=1, source_target_pairs={{0,16},{1,9},{2,18},{3,11},{4,20},{5,13},{6,22},{7,15},{8,24},{9,1... | collective-permute-start | bytes 393224 | tf_op jit(solution)/shard_map/ppermute | solution.py:330
  11.4 14.1 %collective-permute-start.1 = (f32[128,512]{1,0:T(8,128)S(1)}, f32[128,512]{1,0:T(8,128)S(1)}, u32[]{:S(2)}, u32[]{:S(2)}) collective-permute-start(f32[128,512]{1,0:T(8,128)S(1)} %get-tuple-element.17), channel_id=1, source_target_pairs={{0,8},{1,17},{2,10},{3,19},{4,12},{5,21},{6,14},{7,23},{8,0},{9,25... | collective-permute-start | bytes 786440 | tf_op jit(solution)/shard_map/ppermute | solution.py:330
  13.1 12.5 %collective-permute-start.3 = (f32[128,512]{1,0:T(8,128)S(1)}, f32[128,512]{1,0:T(8,128)S(1)}, u32[]{:S(2)}, u32[]{:S(2)}) collective-permute-start(f32[128,512]{1,0:T(8,128)S(1)} %get-tuple-element.19), channel_id=1, source_target_pairs={{0,16},{1,9},{2,18},{3,11},{4,20},{5,13},{6,22},{7,15},{8,24},{9,1... | collective-permute-start | bytes 786440 | tf_op jit(solution)/shard_map/ppermute | solution.py:330
  14.6 11.7 %collective-permute-start.6 = (f32[128,512]{1,0:T(8,128)S(1)}, f32[128,512]{1,0:T(8,128)S(1)}, u32[]{:S(2)}, u32[]{:S(2)}) collective-permute-start(f32[128,512]{1,0:T(8,128)S(1)} %collective-permute-done.4.refs_4_.refs_6_), channel_id=1, source_target_pairs={{0,8},{1,17},{2,10},{3,19},{4,12},{5,21},{6,14},{7,23},{8,0},{9,25... | collective-permute-start | bytes 786440 | tf_op jit(solution)/shard_map/ppermute | solution.py:330
  15.1 11.3 %collective-permute-start.5 = (f32[128,512]{1,0:T(8,128)S(1)}, f32[128,512]{1,0:T(8,128)S(1)}, u32[]{:S(2)}, u32[]{:S(2)}) collective-permute-start(f32[128,512]{1,0:T(8,128)S(1)} %collective-permute-done.refs_1_.refs_3_), channel_id=1, source_target_pairs={{0,16},{1,9},{2,18},{3,11},{4,20},{5,13},{6,22},{7,15},{8,24},{9,1... | collective-permute-start | bytes 786440 | tf_op jit(solution)/shard_map/ppermute | solution.py:330
  17.8 1.3 %collective-permute-start.8 = (f32[32,256]{1,0:T(8,128)S(1)}, f32[32,256]{1,0:T(8,128)S(1)}, u32[]{:S(2)}, u32[]{:S(2)}) collective-permute-start(f32[32,256]{1,0:T(8,128)S(1)} %get-tuple-element.22), channel_id=1, source_target_pairs={{0,1},{1,0},{2,3},{3,2},{4,5},{5,4},{6,7},{7,6},{8,9},{9,8},{10,11... | collective-permute-start | bytes 98312 | tf_op jit(solution)/shard_map/ppermute | solution.py:333
  19.1 4.3 %collective-permute-start.9 = (f32[32,256]{1,0:T(8,128)S(1)}, f32[32,256]{1,0:T(8,128)S(1)}, u32[]{:S(2)}, u32[]{:S(2)}) collective-permute-start(f32[32,256]{1,0:T(8,128)S(1)} %core_sum.1.refs_0_), channel_id=1, source_target_pairs={{0,2},{1,5},{2,0},{3,7},{4,6},{5,1},{6,4},{7,3},{8,10},{9,13},{10,... | collective-permute-start | bytes 98312 | tf_op jit(solution)/shard_map/ppermute | solution.py:337
  23.3 4.8 %collective-permute-start.13 = (f32[32,256]{1,0:T(8,128)S(1)}, f32[32,256]{1,0:T(8,128)S(1)}, u32[]{:S(2)}, u32[]{:S(2)}) collective-permute-start(f32[32,256]{1,0:T(8,128)S(1)} %z_sum.2.refs_7_.refs_0_), channel_id=1, source_target_pairs={{0,4},{1,3},{2,6},{3,1},{4,0},{5,7},{6,2},{7,5},{8,12},{9,11},{10,... | collective-permute-start | bytes 98312 | tf_op jit(solution)/shard_map/ppermute | solution.py:337
  28.2 3.9 %collective-permute-start.14 = (f32[1,32,256]{2,1,0:T(8,128)S(1)}, f32[1,32,256]{2,1,0:T(8,128)S(1)}, u32[]{:S(2)}, u32[]{:S(2)}) collective-permute-start(f32[1,32,256]{2,1,0:T(8,128)S(1)} %bitcast.4), channel_id=1, source_target_pairs={{0,8},{8,0},{16,24},{24,16},{1,9},{9,1},{17,25},{25,17},{2,10},{10... | collective-permute-start | bytes 98312 | tf_op jit(solution)/shard_map/ppermute | solution.py:326
  29.6 3.9 %collective-permute-start.10 = (f32[4,16,1152]{2,1,0:T(8,128)S(1)}, f32[4,16,1152]{2,1,0:T(8,128)S(1)}, u32[]{:S(2)}, u32[]{:S(2)}) collective-permute-start(f32[4,16,1152]{2,1,0:T(8,128)S(1)} %get-tuple-element.24.refs_2_), channel_id=1, source_target_pairs={{0,1},{1,0},{2,3},{3,2},{4,5},{5,4},{6,7},{7,6},{8,9},{9,8},{10,11... | collective-permute-start | bytes 884744 | tf_op jit(solution)/shard_map/ppermute | solution.py:333
  32.1 4.3 %collective-permute-start.15 = (f32[2,32,256]{2,1,0:T(8,128)S(1)}, f32[2,32,256]{2,1,0:T(8,128)S(1)}, u32[]{:S(2)}, u32[]{:S(2)}) collective-permute-start(f32[2,32,256]{2,1,0:T(8,128)S(1)} %stack.2.refs_0_), channel_id=1, source_target_pairs={{0,16},{8,24},{16,0},{24,8},{1,17},{9,25},{17,1},{25,9},{2,18},{10... | collective-permute-start | bytes 196616 | tf_op jit(solution)/shard_map/ppermute | solution.py:326
  33.5 5.7 %collective-permute-start.11 = (f32[2,16,1152]{2,1,0:T(8,128)S(1)}, f32[2,16,1152]{2,1,0:T(8,128)S(1)}, u32[]{:S(2)}, u32[]{:S(2)}) collective-permute-start(f32[2,16,1152]{2,1,0:T(8,128)S(1)} %get-tuple-element.26), channel_id=1, source_target_pairs={{0,2},{1,5},{2,0},{3,7},{4,6},{5,1},{6,4},{7,3},{8,10},{9,13},{10,... | collective-permute-start | bytes 442376 | tf_op jit(solution)/shard_map/ppermute | solution.py:337
  36.4 5.7 %collective-permute-start.16 = (f32[4,32,256]{2,1,0:T(8,128)S(1)}, f32[4,32,256]{2,1,0:T(8,128)S(1)}, u32[]{:S(2)}, u32[]{:S(2)}) collective-permute-start(f32[4,32,256]{2,1,0:T(8,128)S(1)} %stack.3.refs_0_), channel_id=1, source_target_pairs={{0,1},{1,0},{2,3},{3,2},{4,5},{5,4},{6,7},{7,6},{8,9},{9,8},{10,11... | collective-permute-start | bytes 393224 | tf_op jit(solution)/shard_map/ppermute | solution.py:333
  39.2 6.6 %collective-permute-start.12 = (f32[1,16,1152]{2,1,0:T(8,128)S(1)}, f32[1,16,1152]{2,1,0:T(8,128)S(1)}, u32[]{:S(2)}, u32[]{:S(2)}) collective-permute-start(f32[1,16,1152]{2,1,0:T(8,128)S(1)} %get-tuple-element.29), channel_id=1, source_target_pairs={{0,4},{1,3},{2,6},{3,1},{4,0},{5,7},{6,2},{7,5},{8,12},{9,11},{10,... | collective-permute-start | bytes 221192 | tf_op jit(solution)/shard_map/ppermute | solution.py:337
